TPU v7x, 32 devices: a whole 2x2x4 slice. The times are simulated.
32 devices in a mesh: row: 8 (over z, y), col: 2 (over x), depth: 2 (over core).
Axes of the slice: x: 2, y: 2, z: 4, core: 2. Of those that a mesh axis runs over, the one named last changes fastest.
Arguments:
- upper_tiles: bfloat16 [1024, 5, 128, 128], P(('row', 'col')), may hold values from -6 to 6
- upper_cols: int32 [1024, 5], P(('row', 'col')), may hold values from -1 to 1023, as said below
Outputs:
- new_tiles: bfloat16 [1024, 5, 128, 128], P(('row', 'col'), None, 'depth')
Inputs may be any that keep to these rules, and one draw needn't show every extreme that they name: upper_cols[i, o] is (i + o) mod 1024 where block row i holds a block at offset o and -1 where it holds none; offset 0 is always held.
All inputs are finite; a program needn't handle non-finite values.
Results may differ from a plain program's by a relative error of at most 0.0036.
Values may be sent and summed in bfloat16 or wider, within the bound.
A program may use at most 256 MiB of HBM per device.

v0:
```python
import jax
import jax.numpy as jnp
from jax import lax
from jax.sharding import PartitionSpec as P


def passed_along(x, axis, by):
    length = lax.axis_size(axis)
    return lax.ppermute(x, axis, [(i, (i + by) % length) for i in range(length)])


def padded(x, sides, width):
    for axis, dim in sides:
        size, length = (lax.axis_size(axis), x.shape[dim])
        up = [(i, (i + 1) % size) for i in range(size)]
        down = [(j, i) for i, j in up]
        last = lax.slice_in_dim(x, length - width, length, axis=dim)
        leading = lax.slice_in_dim(x, 0, width, axis=dim)
        before = lax.ppermute(last, axis, up)
        after = lax.ppermute(leading, axis, down)
        x = jnp.concatenate([before, x, after], axis=dim)
    return x


def mirror_diagonal(blocks):
    upper_part = jnp.triu(blocks)
    strict_part = jnp.triu(blocks, 1)
    return upper_part + jnp.swapaxes(strict_part, -1, -2)


def whole_rows(stored_ext, first_row, row_count, band_reach):
    lower_part = [
        jnp.swapaxes(
            stored_ext[first_row - shift_by : first_row - shift_by + row_count, shift_by], -1, -2
        )
        for shift_by in range(band_reach, 0, -1)
    ]
    return jnp.concatenate(
        [jnp.stack(lower_part, axis=1), stored_ext[first_row : first_row + row_count]], axis=1
    )


def with_earlier(earlier, stored):
    padding = jnp.zeros((earlier.shape[0], 1) + stored.shape[2:], stored.dtype)
    return jnp.concatenate([jnp.concatenate([padding, earlier], axis=1), stored], axis=0)


def band_product(left_rows, right_ext, low_off, high_off, band_reach):
    row_count = left_rows.shape[0]
    total = jnp.zeros(
        (row_count, high_off - low_off + 1, left_rows.shape[2], right_ext.shape[3]), jnp.float32
    )
    for middle in range(-band_reach, band_reach + 1):
        start_off = max(low_off, middle - band_reach)
        stop_off = min(high_off, middle + band_reach)
        factor = left_rows[:, band_reach + middle]
        partner = right_ext[
            band_reach + middle : band_reach + middle + row_count,
            band_reach + start_off - middle : band_reach + stop_off - middle + 1,
        ]
        term = jnp.einsum("rab,rkbc->rkac", factor, partner, preferred_element_type=jnp.float32)
        total = total.at[:, start_off - low_off : stop_off - low_off + 1].add(term)
    return total


def per_device(upper_tiles, upper_cols):
    row_count = upper_tiles.shape[0]
    band_reach = upper_tiles.shape[1] - 1
    block_size = upper_tiles.shape[2]
    scale_sq = 1.0 / (2.0 * (2 * band_reach + 1) * block_size)
    present = upper_cols >= 0
    masked = jnp.where(present[:, :, None, None], upper_tiles, jnp.zeros_like(upper_tiles))
    stored = jnp.concatenate([mirror_diagonal(masked[:, :1]), masked[:, 1:]], axis=1)
    part_rows = block_size // lax.axis_size("depth")
    part_start = lax.axis_index("depth") * part_rows
    earlier = passed_along(stored[row_count - band_reach :, 1:], ("row", "col"), 1)
    own_rows = whole_rows(with_earlier(earlier, stored), band_reach, row_count, band_reach)
    full_ext = padded(own_rows, ((("row", "col"), 0),), band_reach)
    own_full = full_ext[band_reach : band_reach + row_count]
    left_part = lax.dynamic_slice_in_dim(own_full, part_start, part_rows, 2)
    square_part = (band_product(left_part, full_ext, 0, band_reach, band_reach) * scale_sq).astype(
        jnp.bfloat16
    )
    square = lax.all_gather(square_part, "depth", axis=2, tiled=True)
    earlier_square = passed_along(square[row_count - band_reach :, 1:], ("row", "col"), 1)
    square_rows = whole_rows(
        with_earlier(earlier_square, square), band_reach, row_count, band_reach
    )
    square_ext = padded(square_rows, ((("row", "col"), 0),), band_reach)
    own_part = lax.dynamic_slice_in_dim(own_full, part_start, part_rows, 2)
    product = band_product(own_part, square_ext, 0, band_reach, band_reach)
    linear_term = own_part[:, band_reach:].astype(jnp.float32)
    result = 1.5 * linear_term - 0.5 * product
    result = jnp.where(present[:, :, None, None], result, jnp.float32(0.0))
    return result.astype(jnp.bfloat16)


def solution(mesh):
    placed = (P(("row", "col"), None, None, None), P(("row", "col"), None))
    return jax.shard_map(
        per_device,
        mesh=mesh,
        in_specs=placed,
        out_specs=P(("row", "col"), None, "depth", None),
        check_vma=False,
    )
```

profile of v0, /device:TPU:0, one launch (start us, length us, event | category | flops | bytes accessed | tf_op | source)
XLA Modules:
  0.0 438.0 jit_solution(2834659653881987742)
XLA Ops:
  16.8 10.6 %slice.668 = bf16[64,4,128,128]{3,2,0,1:T(8,128)(2,1)} slice(bf16[64,5,128,128]{3,2,0,1:T(8,128)(2,1)} %copy-done), slice={[0:64], [1:5], [0:128], [0:128]} | slice | bytes 16777216 | tf_op jit(solution)/shard_map/slice | solution.py:73
  37.4 7.1 %fusion.3 = bf16[68,5,128,128]{3,2,0,1:T(8,128)(2,1)S(1)} fusion(bf16[4,4,128,128]{3,2,0,1:T(8,128)(2,1)S(1)} %collective-permute-done, bf16[64,4,128,128]{3,2,0,1:T(8,128)(2,1)} %slice.668, bf16[64,1,128,128]{3,2,0,1:T(8,128)(2,1)S(1)} %copy.6), kind=kLoop, calls=%fused_computation.17 | loop fusion | flops 44564480 | bytes 22151168 | tf_op jit(solution)/shard_map/concatenate | solution.py:45
  77.1 10.4 %constant_dynamic-update-slice_fusion = bf16[64,9,128,128]{3,2,0,1:T(8,128)(2,1)} fusion(bf16[64,9,128,128]{3,2,0,1:T(8,128)(2,1)} %constant_dynamic-update-slice_fusion.1, bf16[64,5,128,128]{3,2,0,1:T(8,128)(2,1)} %copy-done), kind=kLoop, calls=%fused_computation.126 | loop fusion | bytes 16777216 | tf_op jit(solution)/shard_map/concatenate | solution.py:38
  98.0 9.4 %fusion.26 = f32[64,5,128,64]{2,3,0,1:T(8,128)} fusion(bf16[64,4,128,128]{3,2,0,1:T(8,128)(2,1)} %slice.668, bf16[64,1,128,128]{3,2,0,1:T(8,128)(2,1)S(1)} %copy.6, bf16[64,9,128,128]{3,2,0,1:T(8,128)(2,1)} %constant_dynamic-update-slice_fusion, s32[]{:T(128)S(6)} %add.190, s32[]{:T(128)S(6)} %select_n.23), kind=kOutput, calls=%fused_computation.36 | convolution fusion | flops 692060160 | bytes 22020104 | tf_op jit(solution)/shard_map/rab,rkbc->rkac/dot_general | solution.py:61
  107.5 37.2 %collective-permute-done.1 = bf16[4,9,128,128]{3,2,0,1:T(8,128)(2,1)S(1)} collective-permute-done((bf16[4,9,128,128]{3,2,0,1:T(8,128)(2,1)}, bf16[4,9,128,128]{3,2,0,1:T(8,128)(2,1)S(1)}, u32[]{:S(2)}, u32[]{:S(2)}) %collective-permute-start.1) | collective-permute-done | bytes 1179680 | tf_op jit(solution)/shard_map/ppermute | solution.py:19
  152.4 8.6 %fusion.17 = f32[64,5,128,64]{2,3,0,1:T(8,128)} fusion(bf16[64,9,128,128]{3,2,0,1:T(8,128)(2,1)} %constant_dynamic-update-slice_fusion, bf16[4,9,128,128]{3,2,0,1:T(8,128)(2,1)} %collective-permute-done.2, s32[]{:T(128)S(6)} %add.191, s32[]{:T(128)S(6)} %select_n.23), kind=kOutput, calls=%fused_computation.27 | convolution fusion | flops 692060160 | bytes 31588360 | tf_op jit(solution)/shard_map/rab,rkbc->rkac/dot_general | solution.py:61
  161.1 8.6 %fusion.20 = f32[64,5,128,64]{2,3,0,1:T(8,128)} fusion(bf16[64,9,128,128]{3,2,0,1:T(8,128)(2,1)} %constant_dynamic-update-slice_fusion, bf16[4,9,128,128]{3,2,0,1:T(8,128)(2,1)} %collective-permute-done.2, s32[]{:T(128)S(6)} %add.192, s32[]{:T(128)S(6)} %select_n.23), kind=kOutput, calls=%fused_computation.29 | convolution fusion | flops 692060160 | bytes 31588360 | tf_op jit(solution)/shard_map/rab,rkbc->rkac/dot_general | solution.py:61
  169.7 8.6 %fusion.14 = f32[64,5,128,64]{2,3,0,1:T(8,128)} fusion(bf16[64,9,128,128]{3,2,0,1:T(8,128)(2,1)} %constant_dynamic-update-slice_fusion, bf16[4,9,128,128]{3,2,0,1:T(8,128)(2,1)} %collective-permute-done.2, s32[]{:T(128)S(6)} %add.193, s32[]{:T(128)S(6)} %select_n.23), kind=kOutput, calls=%fused_computation.25 | convolution fusion | flops 692060160 | bytes 31588360 | tf_op jit(solution)/shard_map/rab,rkbc->rkac/dot_general | solution.py:61
  178.3 6.8 %fusion.61 = f32[64,5,64,128]{3,2,0,1:T(8,128)} fusion(f32[64,5,64,128]{3,2,0,1:T(8,128)} %scatter-add.26, bf16[64,9,128,128]{3,2,0,1:T(8,128)(2,1)} %constant_dynamic-update-slice_fusion, bf16[4,9,128,128]{3,2,0,1:T(8,128)(2,1)S(1)} %collective-permute-done.1, s32[]{:T(128)S(6)} %add.187, s32[]{:T(128)S(6)} %select_n.23), kind=kOutput, calls=%fused_computation.90 | convolution fusion | flops 277872640 | bytes 29491208 | tf_op jit(solution)/shard_map/rab,rkbc->rkac/dot_general | solution.py:61
  185.1 8.8 %fusion.51 = f32[64,5,64,128]{3,2,0,1:T(8,128)} fusion(f32[64,5,64,128]{3,2,0,1:T(8,128)} %fusion.61, bf16[64,9,128,128]{3,2,0,1:T(8,128)(2,1)} %constant_dynamic-update-slice_fusion, bf16[4,9,128,128]{3,2,0,1:T(8,128)(2,1)S(1)} %collective-permute-done.1, s32[]{:T(128)S(6)} %add.188, s32[]{:T(128)S(6)} %select_n.23), kind=kOutput, calls=%fused_computation.78 | convolution fusion | flops 416808960 | bytes 33685512 | tf_op jit(solution)/shard_map/rab,rkbc->rkac/dot_general | solution.py:61
  193.8 10.0 %fusion.41 = f32[64,5,64,128]{3,2,0,1:T(8,128)} fusion(f32[64,5,64,128]{3,2,0,1:T(8,128)} %fusion.51, bf16[64,9,128,128]{3,2,0,1:T(8,128)(2,1)} %constant_dynamic-update-slice_fusion, bf16[4,9,128,128]{3,2,0,1:T(8,128)(2,1)S(1)} %collective-permute-done.1, s32[]{:T(128)S(6)} %add.189, s32[]{:T(128)S(6)} %select_n.23), kind=kOutput, calls=%fused_computation.66 | convolution fusion | flops 555745280 | bytes 37879816 | tf_op jit(solution)/shard_map/rab,rkbc->rkac/dot_general | solution.py:61
  203.8 24.0 %fusion.35 = bf16[64,5,64,128]{3,2,0,1:T(8,128)(2,1)} fusion(f32[64,5,128,64]{2,3,0,1:T(8,128)} %fusion.14, f32[64,5,128,64]{2,3,0,1:T(8,128)} %fusion.20, f32[64,5,128,64]{2,3,0,1:T(8,128)} %fusion.17, f32[64,5,64,128]{3,2,0,1:T(8,128)} %fusion.41, f32[64,5,128,64]{2,3,0,1:T(8,128)} %fusion.26, bf16[4,9,128,128]{3,2,0,1:T(8,128)(2,1)} %collective-permute-done.2, ...), kind=kOutput, calls=%fused_computation.51 | convolution fusion | flops 710410240 | bytes 78774280 | tf_op jit(solution)/shard_map/rab,rkbc->rkac/dot_general | solution.py:61
  227.9 24.2 %all-gather.2.cloned.1.call-done = bf16[64,5,128,128]{3,2,0,1:T(8,128)(2,1)} async-done(((bf16[64,5,64,128]{3,2,0,1:T(8,128)(2,1)}), bf16[64,5,128,128]{3,2,0,1:T(8,128)(2,1)}) %all-gather.2.cloned.1.call-update) | async-done | bytes 10485776 | tf_op jit(solution)/shard_map/all_gather | solution.py:84
  252.1 14.2 %copy.28 = bf16[64,5,128,128]{2,3,0,1:T(8,128)(2,1)} copy(bf16[64,5,128,128]{3,2,0,1:T(8,128)(2,1)} %all-gather.2.cloned.1.call-done) | data formatting | bytes 20971520 | tf_op jit(solution)/shard_map/all_gather | solution.py:84
  269.2 16.1 %collective-permute-done.3 = bf16[4,4,128,128]{2,3,0,1:T(8,128)(2,1)S(1)} collective-permute-done((bf16[4,4,128,128]{2,3,0,1:T(8,128)(2,1)S(1)}, bf16[4,4,128,128]{2,3,0,1:T(8,128)(2,1)S(1)}, u32[]{:S(2)}, u32[]{:S(2)}) %collective-permute-start.3) | collective-permute-done | bytes 524320 | tf_op jit(solution)/shard_map/ppermute | solution.py:9
  285.2 6.0 %fusion.2 = bf16[68,5,128,128]{2,3,0,1:T(8,128)(2,1)S(1)} fusion(bf16[4,4,128,128]{2,3,0,1:T(8,128)(2,1)S(1)} %collective-permute-done.3, bf16[64,5,128,128]{2,3,0,1:T(8,128)(2,1)} %copy.28), kind=kLoop, calls=%fused_computation.16 | loop fusion | flops 33423360 | bytes 22151168 | tf_op jit(solution)/shard_map/concatenate | solution.py:45
  297.2 12.8 %constant_dynamic-update-slice_fusion.6 = bf16[64,9,128,128]{3,2,0,1:T(8,128)(2,1)} fusion(bf16[64,9,128,128]{3,2,0,1:T(8,128)(2,1)} %fusion.73, bf16[64,5,128,128]{3,2,0,1:T(8,128)(2,1)} %all-gather.2.cloned.1.call-done), kind=kLoop, calls=%fused_computation.132 | loop fusion | bytes 20971520 | tf_op jit(solution)/shard_map/concatenate | solution.py:38
  317.5 9.9 %fusion.82 = f32[64,5,128,64]{2,3,0,1:T(8,128)} fusion(bf16[64,5,128,128]{3,2,0,1:T(8,128)(2,1)} %all-gather.2.cloned.1.call-done, bf16[64,9,128,128]{3,2,0,1:T(8,128)(2,1)} %constant_dynamic-update-slice_fusion, s32[]{:T(128)S(6)} %add.190, s32[]{:T(128)S(6)} %select_n.23), kind=kOutput, calls=%fused_computation.123 | convolution fusion | flops 671088640 | bytes 22020104 | tf_op jit(solution)/shard_map/rab,rkbc->rkac/dot_general | solution.py:61
  327.4 35.0 %collective-permute-done.4 = bf16[4,9,128,128]{3,2,0,1:T(8,128)(2,1)S(1)} collective-permute-done((bf16[4,9,128,128]{3,2,0,1:T(8,128)(2,1)S(1)}, bf16[4,9,128,128]{3,2,0,1:T(8,128)(2,1)S(1)}, u32[]{:S(2)}, u32[]{:S(2)}) %collective-permute-start.4) | collective-permute-done | bytes 1179680 | tf_op jit(solution)/shard_map/ppermute | solution.py:19
  366.3 9.0 %fusion.8 = f32[64,5,128,64]{2,3,0,1:T(8,128)} fusion(bf16[64,9,128,128]{3,2,0,1:T(8,128)(2,1)} %constant_dynamic-update-slice_fusion.6, bf16[4,9,128,128]{3,2,0,1:T(8,128)(2,1)S(1)} %collective-permute-done.5, bf16[64,9,128,128]{3,2,0,1:T(8,128)(2,1)} %constant_dynamic-update-slice_fusion, s32[]{:T(128)S(6)} %add.191, s32[]{:T(128)S(6)} %select_n.23), kind=kOutput, calls=%fused_computation.21 | convolution fusion | flops 692060160 | bytes 31588360 | tf_op jit(solution)/shard_map/rab,rkbc->rkac/dot_general | solution.py:61
  375.3 8.7 %fusion.11 = f32[64,5,128,64]{2,3,0,1:T(8,128)} fusion(bf16[64,9,128,128]{3,2,0,1:T(8,128)(2,1)} %constant_dynamic-update-slice_fusion.6, bf16[4,9,128,128]{3,2,0,1:T(8,128)(2,1)S(1)} %collective-permute-done.5, bf16[64,9,128,128]{3,2,0,1:T(8,128)(2,1)} %constant_dynamic-update-slice_fusion, s32[]{:T(128)S(6)} %add.192, s32[]{:T(128)S(6)} %select_n.23), kind=kOutput, calls=%fused_computation.23 | convolution fusion | flops 692060160 | bytes 31588360 | tf_op jit(solution)/shard_map/rab,rkbc->rkac/dot_general | solution.py:61
  384.0 8.6 %fusion.5 = f32[64,5,128,64]{2,3,0,1:T(8,128)} fusion(bf16[64,9,128,128]{3,2,0,1:T(8,128)(2,1)} %constant_dynamic-update-slice_fusion.6, bf16[4,9,128,128]{3,2,0,1:T(8,128)(2,1)S(1)} %collective-permute-done.5, bf16[64,9,128,128]{3,2,0,1:T(8,128)(2,1)} %constant_dynamic-update-slice_fusion, s32[]{:T(128)S(6)} %add.193, s32[]{:T(128)S(6)} %select_n.23), kind=kOutput, calls=%fused_computation.19 | convolution fusion | flops 692060160 | bytes 31588360 | tf_op jit(solution)/shard_map/rab,rkbc->rkac/dot_general | solution.py:61
  396.6 5.8 %fusion.46 = f32[64,5,64,128]{3,2,0,1:T(8,128)S(1)} fusion(f32[64,5,64,128]{3,2,0,1:T(8,128)S(1)} %fusion.60, bf16[64,9,128,128]{3,2,0,1:T(8,128)(2,1)} %constant_dynamic-update-slice_fusion.6, bf16[4,9,128,128]{3,2,0,1:T(8,128)(2,1)S(1)} %collective-permute-done.4, bf16[64,9,128,128]{3,2,0,1:T(8,128)(2,1)} %constant_dynamic-update-slice_fusion, ...), kind=kOutput, calls=%fused_computation.72 | convolution fusion | flops 416808960 | bytes 33685512 | tf_op jit(solution)/shard_map/rab,rkbc->rkac/dot_general | solution.py:61
  407.5 19.9 %fusion.33 = bf16[64,5,64,128]{3,2,0,1:T(8,128)(2,1)S(1)} fusion(f32[64,5,128,64]{2,3,0,1:T(8,128)} %fusion.5, f32[64,5,128,64]{2,3,0,1:T(8,128)} %fusion.11, f32[64,5,128,64]{2,3,0,1:T(8,128)} %fusion.8, f32[64,5,64,128]{3,2,0,1:T(8,128)S(1)} %fusion.38, f32[64,5,128,64]{2,3,0,1:T(8,128)} %fusion.82, ...), kind=kOutput, calls=%fused_computation.44 | convolution fusion | flops 720896000 | bytes 84019520 | tf_op jit(solution)/shard_map/rab,rkbc->rkac/dot_general | solution.py:61
  (56 shorter events, 103.9 us)
Async XLA Ops:
  6.5 245.6 %all-gather.2.cloned.1.call-start = ((), (), s32[]{:S(2)}) async-start(), calls=%async_computation | async-start | bytes 15728640 | tf_op jit(solution)/shard_map/all_gather | solution.py:84
  7.2 5.7 %copy-start.3 = (pred[64,5]{0,1:T(8,128)(4,1)}, pred[64,5]{0,1:T(8,128)(4,1)S(1)}, u32[]{:S(2)}) copy-start(pred[64,5]{0,1:T(8,128)(4,1)S(1)} %broadcast_compare_fusion) | copy-start | bytes 964
  12.9 3.9 copy-start
  13.0 24.4 %collective-permute-start = (bf16[4,4,128,128]{3,2,0,1:T(8,128)(2,1)S(1)}, bf16[4,4,128,128]{3,2,0,1:T(8,128)(2,1)S(1)}, u32[]{:S(2)}, u32[]{:S(2)}) collective-permute-start(bf16[4,4,128,128]{3,2,0,1:T(8,128)(2,1)S(1)} %slice.666), channel_id=1, source_target_pairs={{0,2},{2,4},{4,6},{6,8},{8,10},{10,12},{12,14},{14,16},{16,18},{18... | collective-permute-start | bytes 1572872 | tf_op jit(solution)/shard_map/ppermute | solution.py:9
  16.8 10.7 %slice-start = ((bf16[64,5,128,128]{3,2,0,1:T(8,128)(2,1)}), bf16[64,1,128,128]{3,2,0,1:T(8,128)(2,1)S(1)}, s32[]{:S(2)}) async-start(bf16[64,5,128,128]{3,2,0,1:T(8,128)(2,1)} %copy-done), calls=%async_computation.1 | async-start | bytes 4194304 | tf_op jit(solution)/shard_map/slice | solution.py:73
  64.4 9.7 %copy-start.2 = (bf16[64,1,128,128]{3,2,0,1:T(8,128)(2,1)S(1)}, bf16[64,1,128,128]{3,2,0,1:T(8,128)(2,1)}, u32[]{:S(2)}) copy-start(bf16[64,1,128,128]{3,2,0,1:T(8,128)(2,1)} %copy.10) | copy-start | bytes 6291460
  90.9 53.8 %collective-permute-start.1 = (bf16[4,9,128,128]{3,2,0,1:T(8,128)(2,1)}, bf16[4,9,128,128]{3,2,0,1:T(8,128)(2,1)S(1)}, u32[]{:S(2)}, u32[]{:S(2)}) collective-permute-start(bf16[4,9,128,128]{3,2,0,1:T(8,128)(2,1)} %get-tuple-element.303), channel_id=1, source_target_pairs={{0,2},{2,4},{4,6},{6,8},{8,10},{10,12},{12,14},{14,16},{16,18},{18... | collective-permute-start | bytes 3538952 | tf_op jit(solution)/shard_map/ppermute | solution.py:19
  93.9 58.6 %collective-permute-start.2 = (bf16[4,9,128,128]{3,2,0,1:T(8,128)(2,1)}, bf16[4,9,128,128]{3,2,0,1:T(8,128)(2,1)}, u32[]{:S(2)}, u32[]{:S(2)}) collective-permute-start(bf16[4,9,128,128]{3,2,0,1:T(8,128)(2,1)} %get-tuple-element.304), channel_id=1, source_target_pairs={{2,0},{4,2},{6,4},{8,6},{10,8},{12,10},{14,12},{16,14},{18,16},{20... | collective-permute-start | bytes 3538952 | tf_op jit(solution)/shard_map/ppermute | solution.py:20
  267.4 17.8 %collective-permute-start.3 = (bf16[4,4,128,128]{2,3,0,1:T(8,128)(2,1)S(1)}, bf16[4,4,128,128]{2,3,0,1:T(8,128)(2,1)S(1)}, u32[]{:S(2)}, u32[]{:S(2)}) collective-permute-start(bf16[4,4,128,128]{2,3,0,1:T(8,128)(2,1)S(1)} %slice.683), channel_id=1, source_target_pairs={{0,2},{2,4},{4,6},{6,8},{8,10},{10,12},{12,14},{14,16},{16,18},{18... | collective-permute-start | bytes 1572872 | tf_op jit(solution)/shard_map/ppermute | solution.py:9
  311.8 50.6 %collective-permute-start.4 = (bf16[4,9,128,128]{3,2,0,1:T(8,128)(2,1)S(1)}, bf16[4,9,128,128]{3,2,0,1:T(8,128)(2,1)S(1)}, u32[]{:S(2)}, u32[]{:S(2)}) collective-permute-start(bf16[4,9,128,128]{3,2,0,1:T(8,128)(2,1)S(1)} %get-tuple-element.301), channel_id=1, source_target_pairs={{0,2},{2,4},{4,6},{6,8},{8,10},{10,12},{12,14},{14,16},{16,18},{18... | collective-permute-start | bytes 3538952 | tf_op jit(solution)/shard_map/ppermute | solution.py:19
  311.9 54.4 %collective-permute-start.5 = (bf16[4,9,128,128]{3,2,0,1:T(8,128)(2,1)S(1)}, bf16[4,9,128,128]{3,2,0,1:T(8,128)(2,1)S(1)}, u32[]{:S(2)}, u32[]{:S(2)}) collective-permute-start(bf16[4,9,128,128]{3,2,0,1:T(8,128)(2,1)S(1)} %get-tuple-element.302), channel_id=1, source_target_pairs={{2,0},{4,2},{6,4},{8,6},{10,8},{12,10},{14,12},{16,14},{18,16},{20... | collective-permute-start | bytes 3538952 | tf_op jit(solution)/shard_map/ppermute | solution.py:20
  366.3 17.7 %copy-start.1 = (bf16[4,9,128,128]{3,2,0,1:T(8,128)(2,1)}, bf16[4,9,128,128]{3,2,0,1:T(8,128)(2,1)S(1)}, u32[]{:S(2)}) copy-start(bf16[4,9,128,128]{3,2,0,1:T(8,128)(2,1)S(1)} %collective-permute-done.5) | copy-start | bytes 3538948
  402.4 5.1 %copy-start.4 = (pred[64,5]{0,1:T(8,128)(4,1)S(1)}, pred[64,5]{0,1:T(8,128)(4,1)}, u32[]{:S(2)}) copy-start(pred[64,5]{0,1:T(8,128)(4,1)} %copy-done.3) | copy-start | bytes 964
Sparse Core Ops, SparseCore 0:
  228.0 24.0 all-gather.1
where the time goes:
time: 446 us; the launch traced here: 438 us
  matrix products  161 us (36%)
  waiting for transfers between devices  112 us (25%)
  local copies, waits for them, and re-layouts  110 us (25%)
  other arithmetic  23.3 us (5%)
  starting transfers between devices  17.6 us (4%)
  between operations  13.8 us (3%)
    dot_general x18, matrix products, band_product(): jnp.einsum('rab,rkbc->rkac', factor, partner, preferred_element_type=jnp....  161 us
    ppermute x2, waiting for transfers between devices, padded(): before = lax.ppermute(last, axis, up)  72.2 us
    all_gather x1, waiting for transfers between devices, per_device(): square = lax.all_gather(square_part, 'depth', axis=2, tiled=True)  24.2 us
    concatenate x2, local copies, waits for them, and re-layouts, whole_rows(): jnp.concatenate([jnp.stack(lower_part, axis=1), stored_ext[first_row:firs...  23.2 us
    another operation x5, local copies, waits for them, and re-layouts, whole_rows(): jnp.stack(lower_part, axis=1)  19.9 us
    unnamed x19, local copies, waits for them, and re-layouts  19.6 us
    ppermute x2, waiting for transfers between devices, passed_along(): lax.ppermute(x, axis, [(i, (i + by) % length) for i in range(length)])  16.1 us
    all_gather x1, local copies, waits for them, and re-layouts, per_device(): square = lax.all_gather(square_part, 'depth', axis=2, tiled=True)  14.2 us
  transfers between devices with their start and end apart: 7, of which 4 were waited for; matrix products, arithmetic and copies ran while one was open for 12% of the time, Pallas kernels for 0%

commit v1 on v0

v1 whole, which is shorter than its diff:
```python
import functools

import jax
import jax.numpy as jnp
from jax import lax
from jax.experimental import pallas as pl
from jax.experimental.pallas import tpu as pltpu
from jax.sharding import PartitionSpec as P

MESH = pl.DeviceIdType.MESH
NT = (((1,), (1,)), ((), ()))
NN = (((1,), (0,)), ((), ()))


def matmul(left, right, dims):
    return lax.dot_general(left, right, dims, preferred_element_type=jnp.float32)


def kernel(
    groups,
    cols_size,
    own_pairs,
    block,
    scale_sq,
    tiles_ref,
    mask_ref,
    out_ref,
    held,
    mask,
    band,
    square,
    staged,
    local_sem,
    mask_sem,
    halo_send,
    halo_recv,
    mask_send,
    mask_recv,
    keep_sem,
    give_send,
    give_recv,
):
    pairs = own_pairs + 4
    wide = 2 * block
    half_rows = 2 * own_pairs
    depth = lax.axis_index("depth")
    place = lax.axis_index("row") * cols_size + lax.axis_index("col")
    after = lax.rem(place + 1, groups)
    before = lax.rem(place + groups - 1, groups)

    def device(group, layer):
        return (group // cols_size, lax.rem(group, cols_size), layer)

    barrier = pltpu.get_barrier_semaphore()
    for other in (device(after, depth), device(before, depth), device(place, 1 - depth)):
        pl.semaphore_signal(barrier, inc=1, device_id=other, device_id_type=MESH)

    local_count = half_rows + 4
    local_from = depth * (half_rows - 4)
    local_to = 4 * (1 - depth)
    own_copy = pltpu.make_async_copy(
        tiles_ref.at[pl.ds(local_from, local_count)],
        held.at[pl.ds(local_to, local_count)],
        local_sem,
    )
    own_copy.start()
    own_mask = pltpu.make_async_copy(
        mask_ref.at[pl.ds(local_from, local_count)],
        mask.at[pl.ds(local_to, local_count)],
        mask_sem,
    )
    own_mask.start()
    pl.semaphore_wait(barrier, 3)

    partner = jnp.where(depth == 0, after, before)
    give_from = (1 - depth) * (2 * half_rows - 4)
    give_to = depth * (half_rows + 4)
    halo = pltpu.make_async_remote_copy(
        src_ref=tiles_ref.at[pl.ds(give_from, 4)],
        dst_ref=held.at[pl.ds(give_to, 4)],
        send_sem=halo_send,
        recv_sem=halo_recv,
        device_id=device(partner, depth),
        device_id_type=MESH,
    )
    halo.start()
    halo_mask = pltpu.make_async_remote_copy(
        src_ref=mask_ref.at[pl.ds(give_from, 4)],
        dst_ref=mask.at[pl.ds(give_to, 4)],
        send_sem=mask_send,
        recv_sem=mask_recv,
        device_id=device(partner, depth),
        device_id_type=MESH,
    )
    halo_mask.start()
    own_mask.wait()
    own_copy.wait()

    def spread(pair, carry):
        zero = jnp.zeros((block, block), jnp.bfloat16)
        band[pair, 0:block, 9 * block : 10 * block] = zero
        band[pair, block:wide, 0:block] = zero
        for a in range(2):
            for o in range(5):
                values = held[2 * pair + a, o].astype(jnp.float32)
                present = mask[2 * pair + a, o : o + 1, :]
                values = jnp.where(present > 0, values, 0.0)
                if o == 0:
                    down = lax.broadcasted_iota(jnp.int32, (block, block), 0)
                    along = lax.broadcasted_iota(jnp.int32, (block, block), 1)
                    values = jnp.where(down <= along, values, values.T)
                values = values.astype(jnp.bfloat16)
                at = (a + o + 4) * block
                band[pair, a * block : (a + 1) * block, at : at + block] = values
                if o > 0:
                    step, b = divmod(a + o, 2)
                    at = (a - 2 * step + 4) * block
                    band[pair + step, b * block : (b + 1) * block, at : at + block] = values.T
        return carry

    def square_tile(pair, e):
        total = matmul(band[pair, :, e * wide :], band[pair + e, :, : (5 - e) * wide], NT)
        tile = (total * scale_sq).astype(jnp.bfloat16)
        square[pair, :, e * wide : (e + 1) * wide] = tile
        if e == 2:
            square[pair, 0:block, 5 * block : 6 * block] = jnp.zeros((block, block), jnp.bfloat16)

    def square_row(pair, carry):
        for e in range(3):
            square_tile(pair, e)
        return carry

    def keep(own):
        rows = pl.ds(2 * own, 2)
        return pltpu.make_async_copy(
            staged.at[rows, :, depth],
            out_ref.at[pl.ds(depth * half_rows + 2 * own, 2)],
            keep_sem.at[own],
        )

    def give(own):
        rows = pl.ds(2 * own, 2)
        return pltpu.make_async_remote_copy(
            src_ref=staged.at[rows, :, 1 - depth],
            dst_ref=out_ref.at[pl.ds(depth * half_rows + 2 * own, 2)],
            send_sem=give_send.at[own],
            recv_sem=give_recv.at[own],
            device_id=device(place, 1 - depth),
            device_id_type=MESH,
        )

    def out_row(own, carry):
        pair = own + 2
        for e in range(3):
            k = pair + e
            total = matmul(band[pair, :, (e + 2) * wide :], square[k, :, : (3 - e) * wide], NT)
            total += matmul(
                band[pair, :, e * wide : (e + 1) * wide], square[k - 2, :, 2 * wide : 3 * wide], NN
            )
            total += matmul(
                band[pair, :, (e + 1) * wide : (e + 2) * wide], square[k - 1, :, wide : 2 * wide], NN
            )
            for a in range(2):
                for b in range(2):
                    o = 2 * e + b - a
                    if 0 <= o <= 4:
                        product = total[a * block : (a + 1) * block, b * block : (b + 1) * block]
                        at = (a + o + 4) * block
                        linear = band[pair, a * block : (a + 1) * block, at : at + block]
                        value = 1.5 * linear.astype(jnp.float32) - 0.5 * product
                        present = mask[2 * pair + a, o : o + 1, :]
                        value = jnp.where(present > 0, value, 0.0).astype(jnp.bfloat16)
                        for part in range(2):
                            staged[2 * own + a, o, part] = value[
                                part * block // 2 : (part + 1) * block // 2
                            ]
        keep(own).start()
        give(own).start()
        return carry

    low = 2 * (1 - depth)
    lax.fori_loop(low, low + own_pairs + 2, spread, 0)
    lax.fori_loop(2 + low, own_pairs + low, square_row, 0)
    halo.wait()
    halo_mask.wait()
    late = depth * (own_pairs + 2)
    lax.fori_loop(late, late + 2, spread, 0)
    late_square = 2 + depth * (own_pairs - 2)
    lax.fori_loop(late_square, late_square + 2, square_row, 0)
    for pair, e in ((0, 2), (1, 1), (1, 2)):
        square_tile(pair, e)
    for pair, e in ((2, 0), (2, 1), (3, 0)):
        square_tile(own_pairs + pair, e)
    lax.fori_loop(0, own_pairs, out_row, 0)

    def finish(own, carry):
        keep(own).wait()
        give(own).wait()
        return carry

    lax.fori_loop(0, own_pairs, finish, 0)


def per_device(upper_tiles, upper_cols):
    rows, offsets, block, _ = upper_tiles.shape
    reach = offsets - 1
    scale_sq = 1.0 / (2.0 * (2 * reach + 1) * block)
    cols_size = lax.axis_size("col")
    groups = lax.axis_size("row") * cols_size
    own_pairs = rows // 4
    pairs = own_pairs + 4
    present = (upper_cols >= 0).astype(jnp.float32)
    present = jnp.pad(present, ((0, 0), (0, 8 - offsets)))
    present = jnp.broadcast_to(present[:, :, None], (rows, 8, 128))
    body = functools.partial(kernel, groups, cols_size, own_pairs, block, scale_sq)
    dma = pltpu.SemaphoreType.DMA
    return pl.pallas_call(
        body,
        out_shape=jax.ShapeDtypeStruct((rows, offsets, block // 2, block), jnp.bfloat16),
        in_specs=[pl.BlockSpec(memory_space=pl.ANY)] * 2,
        out_specs=pl.BlockSpec(memory_space=pl.ANY),
        scratch_shapes=[
            pltpu.VMEM((2 * pairs, offsets, block, block), jnp.bfloat16),
            pltpu.VMEM((2 * pairs, 8, 128), jnp.float32),
            pltpu.VMEM((pairs + 2, 2 * block, 10 * block), jnp.bfloat16),
            pltpu.VMEM((pairs, 2 * block, 6 * block), jnp.bfloat16),
            pltpu.VMEM((2 * own_pairs, offsets, 2, block // 2, block), jnp.bfloat16),
            dma,
            dma,
            dma,
            dma,
            dma,
            dma,
            dma((own_pairs,)),
            dma((own_pairs,)),
            dma((own_pairs,)),
        ],
        compiler_params=pltpu.CompilerParams(
            collective_id=0, has_side_effects=True, vmem_limit_bytes=56 * 1024 * 1024
        ),
        cost_estimate=pl.CostEstimate(
            flops=14_000_000_000, bytes_accessed=20_000_000, transcendentals=0
        ),
    )(upper_tiles, present)


def solution(mesh):
    placed = (P(("row", "col"), None, None, None), P(("row", "col"), None))
    return jax.shard_map(
        per_device,
        mesh=mesh,
        in_specs=placed,
        out_specs=P(("row", "col"), None, "depth", None),
        check_vma=False,
    )
```

time: 446 us -> 41.3 us (0.09); the launches traced: 438 us -> 40.9 us
  matrix products: 161 us -> 0 us
  waiting for transfers between devices: 112 us -> 0 us
  local copies, waits for them, and re-layouts: 110 us -> 7.04 us
  Pallas kernels: 0 us -> 33.2 us
  other arithmetic: 23.3 us -> 0.7 us
  starting transfers between devices: 17.6 us -> 0 us
  between operations: 13.8 us -> 0.01 us
    dot_general x18 -> x0, matrix products: 161 us -> none  [band_product(): jnp.einsum('rab,rkbc->rkac', factor, partner, preferred_element_type=jnp....]
    ppermute x6 -> x0, waiting for transfers between devices: 88.2 us -> none  [the longest x2 72.2 us: padded(): before = lax.ppermute(last, axis, up)]
    pallas_call x0 -> x1, Pallas kernels: none -> 33.2 us  [per_device(): pl.pallas_call(body, out_shape=jax.ShapeDtypeStruct((rows, offsets, block...]
    all_gather x1 -> x0, waiting for transfers between devices: 24.2 us -> none  [per_device(): square = lax.all_gather(square_part, 'depth', axis=2, tiled=True)]
    concatenate x2 -> x0, local copies, waits for them, and re-layouts: 23.2 us -> none  [whole_rows(): jnp.concatenate([jnp.stack(lower_part, axis=1), stored_ext[first_row:firs...]
    another operation x5 -> x0, local copies, waits for them, and re-layouts: 19.9 us -> none  [whole_rows(): jnp.stack(lower_part, axis=1)]
    slice x8 -> x0, local copies, waits for them, and re-layouts: 19.8 us -> none  [the longest x1 10.6 us: per_device(): masked[:, 1:]]
    ppermute x6 -> x0, starting transfers between devices: 17.6 us -> none  [the longest x2 9.8 us: padded(): after = lax.ppermute(leading, axis, down)]
  transfers between devices with their start and end apart: 7 -> 0, of which waited for: 4 -> 0; matrix products, arithmetic and copies ran while one was open for 12% -> 0% of each run, Pallas kernels for 0% -> 0%
where the time goes in v1:
time: 41.3 us; the launch traced here: 40.9 us
  Pallas kernels  33.2 us (80%)
  local copies, waits for them, and re-layouts  7.04 us (17%)
  other arithmetic  0.7 us (2%)
    pallas_call x1, Pallas kernels, per_device(): pl.pallas_call(body, out_shape=jax.ShapeDtypeStruct((rows, offsets, block...  33.2 us
    unnamed x1, local copies, waits for them, and re-layouts  6.11 us
    broadcast_in_dim x1, local copies, waits for them, and re-layouts, per_device(): present = jnp.broadcast_to(present[:, :, None], (rows, 8, 128))  0.84 us

profile of v1, /device:TPU:0, one launch (start us, length us, event | category | flops | bytes accessed | tf_op | source)
XLA Modules:
  0.0 40.9 jit_solution(14376105724981634485)
XLA Ops:
  0.0 0.7 %broadcast_compare_fusion = pred[64,5]{0,1:T(8,128)(4,1)S(1)} fusion(s32[64,5]{0,1:T(8,128)} %param.3), kind=kLoop, calls=%fused_computation.1 | loop fusion | flops 320 | bytes 1600 | tf_op jit(solution)/shard_map/ge | solution.py:212
  0.7 0.1 copy.3
  0.8 0.8 %broadcast_in_dim.2.mask_ref = f32[64,8,128]{2,1,0:T(8,128)} broadcast(f32[64,8]{1,0:T(8,128)S(1)} %copy.3), dimensions={0,1} | broadcast | bytes 264192 | tf_op jit(solution)/shard_map/broadcast_in_dim | solution.py:214
  1.6 33.2 %shard_map.28 = bf16[64,5,64,128]{3,2,1,0:T(8,128)(2,1)} custom-call(bf16[64,5,128,128]{3,2,1,0:T(8,128)(2,1)} %tiles_ref.1, f32[64,8,128]{2,1,0:T(8,128)} %broadcast_in_dim.2.mask_ref), custom_call_target="tpu_custom_call" | custom-call | flops 14000000000 | bytes 20000000 | tf_op jit(solution)/shard_map/pallas_call | solution.py:217
  34.8 6.1 %copy.5 = bf16[64,5,64,128]{3,2,1,0:T(8,128)(2,1)} copy(bf16[64,5,64,128]{3,2,1,0:T(8,128)(2,1)} %shard_map.28) | data formatting | bytes 10485760
  (1 shorter events, 0.0 us)
